TPU v7x, 256 devices: a whole 4x4x8 slice. The times are simulated.
256 devices in a mesh: prow: 32 (over z_hi, x, y), pcol: 8 (over z_lo, core).
Axes of the slice: x: 4, y: 4, z: 8 (z_hi: 2, z_lo: 4; z = z_hi * 4 + z_lo), core: 2. Of those that a mesh axis runs over, the one named last changes fastest.
Arguments:
- inverse: bfloat16 [2, 4096, 4096], P(None, 'pcol', 'prow'), may hold values from -0.09375 to 0.09375
- coupling: bfloat16 [4096, 4096], P('prow', 'pcol'), may hold values from -0.09375 to 0.09375
- panel: bfloat16 [2, 49152, 4096], P(None, 'prow', 'pcol'), may hold values from -0.0625 to 0.0625
- modes: bfloat16 [2, 512, 4096], P(None, 'prow', 'pcol'), may hold values from -0.0625 to 0.0625
- rhs_window: bfloat16 [2, 4096, 1024], P(None, ('prow', 'pcol')), may hold values from -6 to 6
- rhs_above: bfloat16 [49152, 1024], P(('prow', 'pcol')), may hold values from -6 to 6
Outputs:
- potential: bfloat16 [2, 4096, 1024], P(None, ('pcol', 'prow'))
- above_rows: float32 [49152, 1024], P(('prow', 'pcol'))
- forces: float32 [512, 1024], P(('prow', 'pcol'))
All inputs are finite; a program needn't handle non-finite values.
Results may differ from a plain program's by a relative error of at most 0.02.
Values may be sent and summed in bfloat16 or wider, within the bound.
A program may use at most 64 MiB of HBM per device.

v0:
```python
import jax
import jax.numpy as jnp
from jax import lax
from jax.sharding import PartitionSpec as P


def body(inverse, coupling, panel, modes, rhs_window, rhs_above):

    def solve_block(rhs_local, block_index):
        across = lax.all_gather(rhs_local, "pcol", axis=0, tiled=True)
        picked = inverse[block_index]
        return lax.psum_scatter(
            jnp.dot(picked, across, preferred_element_type=jnp.float32),
            "prow",
            scatter_dimension=0,
            tiled=True,
        ).astype(jnp.bfloat16)

    def spread(solved):
        return lax.all_gather(solved, "prow", axis=0, tiled=True)

    def panel_term(block_index, columns):
        picked = panel[block_index]
        return jnp.dot(picked, columns, preferred_element_type=jnp.float32)

    second_block = solve_block(rhs_window[1], 1)
    second_all = spread(second_block)
    update_second = lax.psum_scatter(
        panel_term(1, second_all).astype(jnp.bfloat16), "pcol", scatter_dimension=0, tiled=True
    ).astype(jnp.float32)
    picked = coupling
    carried = lax.psum_scatter(
        jnp.dot(picked, second_all, preferred_element_type=jnp.float32).astype(jnp.bfloat16),
        "pcol",
        scatter_dimension=0,
        tiled=True,
    ).astype(jnp.float32)
    reduced = (rhs_window[0].astype(jnp.float32) - carried).astype(jnp.bfloat16)
    first_block = solve_block(reduced, 0)
    first_all = spread(first_block)
    update_first = lax.psum_scatter(
        panel_term(0, first_all).astype(jnp.bfloat16), "pcol", scatter_dimension=0, tiled=True
    ).astype(jnp.float32)
    above_rows = rhs_above.astype(jnp.float32) - update_second - update_first
    mode_terms = jnp.dot(modes[0], first_all, preferred_element_type=jnp.float32) + jnp.dot(
        modes[1], second_all, preferred_element_type=jnp.float32
    )
    forces = lax.psum_scatter(
        mode_terms.astype(jnp.bfloat16), "pcol", scatter_dimension=0, tiled=True
    ).astype(jnp.float32)
    potential = jnp.stack([first_block, second_block])
    return (potential, above_rows, forces)


def solution(mesh):
    placed = (
        P(None, "pcol", "prow"),
        P("prow", "pcol"),
        P(None, "prow", "pcol"),
        P(None, "prow", "pcol"),
        P(None, ("prow", "pcol"), None),
        P(("prow", "pcol"), None),
    )
    return jax.shard_map(
        body,
        mesh=mesh,
        in_specs=placed,
        out_specs=(
            P(None, ("pcol", "prow"), None),
            P(("prow", "pcol"), None),
            P(("prow", "pcol"), None),
        ),
        check_vma=False,
    )
```

profile of v0, /device:TPU:1, one launch (start us, length us, event | category | flops | bytes accessed | tf_op | source)
XLA Modules:
  0.0 791.8 jit_solution(7514812416540917769)
XLA Ops:
  7.2 0.0 copy-start
  7.2 0.0 reduce-scatter.10.cloned.1.call-start
  7.2 0.8 slice.26
  8.0 17.3 %all-gather = bf16[1,128,1024]{2,1,0:T(8,128)(2,1)S(1)} all-gather(bf16[1,16,1024]{2,1,0:T(8,128)(2,1)S(1)} %slice.26), channel_id=2, replica_groups=mesh['prow'=32,'pcol'=8] {'pcol'}, dimensions={1}, use_global_device_ids=true | all-gather | bytes 294912 | tf_op jit(solution)/shard_map/all_gather | solution.py:10
  25.3 2.7 fusion.9
  28.0 0.0 reduce-scatter.10.cloned.1.call-update
  28.0 0.0 all-gather.4.cloned.1.call-start
  28.1 205.1 %reduce-scatter.10.cloned.1.call-done = f32[16,1024]{1,0:T(8,128)} async-done(((f32[512,1024]{1,0:T(8,128)}), f32[16,1024]{1,0:T(8,128)}) %reduce-scatter.10.cloned.1.call-update) | async-done | bytes 65552 | tf_op jit(solution)/shard_map/reduce_scatter | solution.py:12
  233.2 1.5 convert_element_type.56
  234.6 0.0 all-gather.4.cloned.1.call-update
  234.7 0.0 reduce-scatter.12.cloned.1.call-start
  234.7 101.0 %all-gather.4.cloned.1.call-done = bf16[512,1024]{1,0:T(8,128)(2,1)} async-done(((bf16[16,1024]{1,0:T(8,128)(2,1)}), bf16[512,1024]{1,0:T(8,128)(2,1)}) %all-gather.4.cloned.1.call-update) | async-done | bytes 1048592 | tf_op jit(solution)/shard_map/all_gather | solution.py:20
  335.7 2.3 fusion.6
  338.0 0.0 reduce-scatter.12.cloned.1.call-update
  338.0 0.0 reduce-scatter.14.cloned.1.call-start
  338.1 29.0 %reduce-scatter.12.cloned.1.call-done = bf16[16,1024]{1,0:T(8,128)(2,1)} async-done(((bf16[128,1024]{1,0:T(8,128)(2,1)}), bf16[16,1024]{1,0:T(8,128)(2,1)}) %reduce-scatter.12.cloned.1.call-update) | async-done | bytes 32784 | tf_op jit(solution)/shard_map/reduce_scatter | solution.py:32
  367.1 0.8 fusion.15
  367.9 17.8 %all_gather.14 = bf16[128,1024]{1,0:T(8,128)(2,1)S(1)} all-gather(bf16[16,1024]{1,0:T(8,128)(2,1)S(1)} %fusion.15), channel_id=1, replica_groups=mesh['prow'=32,'pcol'=8] {'pcol'}, dimensions={0}, use_global_device_ids=true | all-gather | bytes 294912 | tf_op jit(solution)/shard_map/all_gather | solution.py:10
  385.7 1.7 convolution_bitcast_fusion
  387.5 0.0 reduce-scatter.14.cloned.1.call-update
  387.5 0.0 all-gather.6.cloned.1.call-start
  387.6 202.6 %reduce-scatter.14.cloned.1.call-done = f32[16,1024]{1,0:T(8,128)} async-done(((f32[512,1024]{1,0:T(8,128)}), f32[16,1024]{1,0:T(8,128)}) %reduce-scatter.14.cloned.1.call-update) | async-done | bytes 65552 | tf_op jit(solution)/shard_map/reduce_scatter | solution.py:12
  590.1 1.5 convert_element_type.61
  591.6 0.0 all-gather.6.cloned.1.call-update
  591.6 0.0 reduce-scatter.16.cloned.1.call-start
  591.7 4.9 fusion
  596.6 4.7 copy.16
  601.3 0.0 reduce-scatter.16.cloned.1.call-update
  601.3 0.0 reduce-scatter.18.cloned.1.call-start
  601.4 91.2 %all-gather.6.cloned.1.call-done = bf16[512,1024]{1,0:T(8,128)(2,1)} async-done(((bf16[16,1024]{1,0:T(8,128)(2,1)}), bf16[512,1024]{1,0:T(8,128)(2,1)}) %all-gather.6.cloned.1.call-update) | async-done | bytes 1048592 | tf_op jit(solution)/shard_map/all_gather | solution.py:20
  692.6 5.3 fusion.1
  697.9 4.7 copy.18
  702.6 0.0 copy-start.8
  702.6 0.0 reduce-scatter.18.cloned.1.call-update
  702.6 0.9 copy-done.3
  703.6 0.2 copy.13
  703.8 0.6 dynamic-slice
  705.1 0.6 pad_maximum_fusion
  705.7 28.2 %reduce-scatter.16.cloned.1.call-done = bf16[192,1024]{1,0:T(8,128)(2,1)} async-done(((bf16[1536,1024]{1,0:T(8,128)(2,1)}), bf16[192,1024]{1,0:T(8,128)(2,1)}) %reduce-scatter.16.cloned.1.call-update) | async-done | bytes 393232
  733.9 1.2 copy.17
  735.2 0.3 fusion.17
  735.4 0.3 fusion.8
  735.7 26.7 %all-reduce = bf16[16,1024]{1,0:T(8,128)(2,1)S(1)} all-reduce(bf16[16,1024]{1,0:T(8,128)(2,1)S(1)} %fusion.8), channel_id=8, replica_groups=mesh['prow'=32,'pcol'=8] {'pcol'}, use_global_device_ids=true, to_apply=%region_5.0.clone | all-reduce | flops 16384 | bytes 65536
  762.4 0.6 dynamic-slice_convert_fusion
  763.0 19.4 %reduce-scatter.18.cloned.1.call-done = bf16[192,1024]{1,0:T(8,128)(2,1)} async-done(((bf16[1536,1024]{1,0:T(8,128)(2,1)}), bf16[192,1024]{1,0:T(8,128)(2,1)}) %reduce-scatter.18.cloned.1.call-update) | async-done | bytes 393232
  782.4 1.2 copy.19
  783.6 0.2 convert_subtract_fusion
  783.8 1.2 copy.14
  (19 shorter events, 0.0 us)
Async XLA Ops:
  7.2 328.5 %copy-start = (bf16[128,512]{1,0:T(8,128)(2,1)S(1)}, bf16[128,512]{1,0:T(8,128)(2,1)}, u32[]{:S(2)}) copy-start(bf16[128,512]{1,0:T(8,128)(2,1)} %param.7) | copy-start | bytes 393220
  7.2 226.0 %reduce-scatter.10.cloned.1.call-start = ((), (), s32[]{:S(2)}) async-start(), calls=%async_computation.5 | async-start | bytes 2162688 | tf_op jit(solution)/shard_map/reduce_scatter | solution.py:12
  25.3 341.8 %copy-start.7 = (bf16[2,16,1024]{2,1,0:T(8,128)(2,1)S(1)}, bf16[2,16,1024]{2,1,0:T(8,128)(2,1)}, u32[]{:S(2)}) copy-start(bf16[2,16,1024]{2,1,0:T(8,128)(2,1)} %param.10) | copy-start | bytes 196612
  25.3 360.5 %copy-start.4 = (bf16[2,512,128]{2,1,0:T(8,128)(2,1)S(1)}, bf16[2,512,128]{2,1,0:T(8,128)(2,1)}, u32[]{:S(2)}) copy-start(bf16[2,512,128]{2,1,0:T(8,128)(2,1)} %param.6) | copy-start | bytes 786436
  28.0 307.7 %all-gather.4.cloned.1.call-start = ((), (), s32[]{:S(2)}) async-start(), calls=%async_computation.6 | async-start | bytes 1081344 | tf_op jit(solution)/shard_map/all_gather | solution.py:20
  234.7 132.5 %reduce-scatter.12.cloned.1.call-start = ((), (), s32[]{:S(2)}) async-start(), calls=%async_computation.7 | async-start | bytes 294912 | tf_op jit(solution)/shard_map/reduce_scatter | solution.py:32
  335.7 256.0 %copy-start.1 = (bf16[512,1024]{1,0:T(8,128)(2,1)S(1)}, bf16[512,1024]{1,0:T(8,128)(2,1)}, u32[]{:S(2)}) copy-start(bf16[512,1024]{1,0:T(8,128)(2,1)} %all-gather.4.cloned.1.call-done) | copy-start | bytes 3145732
  338.0 252.1 %reduce-scatter.14.cloned.1.call-start = ((), (), s32[]{:S(2)}) async-start(), calls=%async_computation.8 | async-start | bytes 2162688 | tf_op jit(solution)/shard_map/reduce_scatter | solution.py:12
  387.5 305.1 %all-gather.6.cloned.1.call-start = ((), (), s32[]{:S(2)}) async-start(), calls=%async_computation.9 | async-start | bytes 1081344 | tf_op jit(solution)/shard_map/all_gather | solution.py:20
  591.6 142.3 %reduce-scatter.16.cloned.1.call-start = ((), (), s32[]{:S(2)}) async-start(), calls=%async_computation.10 | async-start | bytes 3538944
  601.3 181.1 %reduce-scatter.18.cloned.1.call-start = ((), (), s32[]{:S(2)}) async-start(), calls=%async_computation.11 | async-start | bytes 3538944
  702.6 1.0 copy-start.3
  702.6 1.2 copy-start.9
  702.6 2.5 copy-start.5
  702.6 2.5 copy-start.6
  702.6 32.6 %copy-start.2 = (bf16[512,1024]{1,0:T(8,128)(2,1)S(1)}, bf16[512,1024]{1,0:T(8,128)(2,1)}, u32[]{:S(2)}) copy-start(bf16[512,1024]{1,0:T(8,128)(2,1)} %all-gather.6.cloned.1.call-done) | copy-start | bytes 3145732
  702.6 32.6 %copy-start.8 = (bf16[2,16,512]{2,1,0:T(8,128)(2,1)S(1)}, bf16[2,16,512]{2,1,0:T(8,128)(2,1)}, u32[]{:S(2)}) copy-start(bf16[2,16,512]{2,1,0:T(8,128)(2,1)} %param.9) | copy-start | bytes 98308
Sparse Core Ops, SparseCore 0:
  28.2 204.9 reduce-scatter.9
  237.7 97.9 all-gather.3
  338.9 28.1 reduce-scatter.11
  387.6 202.4 reduce-scatter.13
  594.5 98.0 all-gather.5
  695.2 38.7 reduce-scatter.15
  736.7 45.6 reduce-scatter.17
where the time goes:
time: 794 us; the launch traced here: 792 us
  waiting for transfers between devices  677 us (85%)
  blocking collectives  61.8 us (8%)
  matrix products  17.5 us (2%)
  local copies, waits for them, and re-layouts  15.5 us (2%)
  between operations  14.9 us (2%)
    reduce_scatter x2, waiting for transfers between devices, solve_block(): lax.psum_scatter(jnp.dot(picked, across, preferred_element_type=jnp.float...  408 us
    all_gather x2, waiting for transfers between devices, spread(): return lax.all_gather(solved, 'prow', axis=0, tiled=True)  192 us
    unnamed x9, waiting for transfers between devices  47.8 us
    all_gather x2, blocking collectives, solve_block(): across = lax.all_gather(rhs_local, 'pcol', axis=0, tiled=True)  35.1 us
    reduce_scatter x1, waiting for transfers between devices, body(): lax.psum_scatter(jnp.dot(picked, second_all, preferred_element_type=jnp.f...  29 us
    unnamed x1, blocking collectives  26.7 us
  transfers between devices with their start and end apart: 7, of which 7 were waited for; matrix products, arithmetic and copies ran while one was open for 3% of the time, Pallas kernels for 0%

commit v1 on v0

v1 whole, which is shorter than its diff:
```python
import functools

import jax
import jax.numpy as jnp
from jax import lax
from jax.experimental import pallas as pl
from jax.experimental.pallas import tpu as pltpu
from jax.sharding import PartitionSpec as P

MESH = pl.DeviceIdType.MESH
CHUNKS = 4
SKEW = 0.0
N_SEMS = 4 * 60 + 16
BF16 = jnp.bfloat16
F32 = jnp.float32


def kernel(
    inv_ref, coup_ref, panel_ref, modes_ref, rhsw_ref, rhsa_ref,
    pot_ref, above_ref, forces_ref,
    g, part, r1, part2, r2, part3, r3, xs, cpart, cr1, cp2, cr2,
    fpart, fr1, fp2, fr2, fo, fot, fob, fob1, fo2, fo2r, fin,
    send_sems, recv_sems,
):
    w = g.shape[-1]
    row = lax.axis_index("prow")
    col = lax.axis_index("pcol")
    h, x, y = row // 16, (row // 4) % 4, row % 4
    zl, k = col // 2, col % 2

    def at_x(d):
        return (h * 16 + ((x + d) % 4) * 4 + y, col)

    def at_y(d):
        return (h * 16 + x * 4 + (y + d) % 4, col)

    def at_z(d):
        return (row, ((zl + d) % 4) * 2 + k)

    at_h = ((1 - h) * 16 + x * 4 + y, col)
    sibling = (row, zl * 2 + 1 - k)

    barrier = pltpu.get_barrier_semaphore()
    partners = [at_x(d) for d in (1, 2, 3)] + [at_y(d) for d in (1, 2, 3)]
    partners += [at_z(d) for d in (1, 2, 3)] + [at_h, sibling]
    for partner in partners:
        pl.semaphore_signal(barrier, inc=1, device_id=partner, device_id_type=MESH)
    pl.semaphore_wait(barrier, len(partners))

    sent = []
    pending = {}

    def send(key, src, dst, device):
        i = len(sent)
        copy = pltpu.make_async_remote_copy(
            src_ref=src, dst_ref=dst, send_sem=send_sems.at[i], recv_sem=recv_sems.at[i],
            device_id=device, device_id_type=MESH,
        )
        copy.start()
        sent.append(copy)
        pending.setdefault(key, []).append(copy)

    def arrived(key):
        for copy in pending.pop(key):
            copy.wait_recv()

    def cols(j):
        return pl.ds(j * w, w)

    def first_axis(j):
        return "y" if j % 2 == 0 else "x"

    def gather_z(b, j):
        for d in (1, 2, 3):
            send(("gz", b, j), g.at[b, j, zl, k], g.at[b, j, zl, k], at_z(d))

    def load_rhs(j):
        g[1, j, zl, k] = rhsw_ref[1, :, cols(j)]
        gather_z(1, j)

    def gather_core(b, j):
        arrived(("gz", b, j))
        send(("gc", b, j), g.at[b, j, :, k], g.at[b, j, :, k], sibling)

    def solve(b, j):
        arrived(("gc", b, j))
        right = g[b, j].reshape(128, w)

        def tile(t, carry):
            rows = inv_ref[b, pl.ds(pl.multiple_of(t * 128, 128), 128), :]
            value = jnp.dot(rows, right, preferred_element_type=F32).astype(BF16)
            part[b, j, t // 2, pl.ds((t % 2) * 2, 2)] = value.reshape(2, 4, 16, w)
            return carry

        lax.fori_loop(0, 4, tile, 0)
        for d in (1, 2, 3):
            if first_axis(j) == "y":
                send(("r1", b, j), part.at[b, j, :, :, (y + d) % 4], r1.at[b, j, d - 1], at_y(d))
            else:
                send(("r1", b, j), part.at[b, j, :, (x + d) % 4], r1.at[b, j, d - 1], at_x(d))

    def reduce_second(b, j):
        arrived(("r1", b, j))
        own = part[b, j, :, :, y] if first_axis(j) == "y" else part[b, j, :, x]
        total = own.astype(F32) + r1[b, j, 0].astype(F32)
        total = total + r1[b, j, 1].astype(F32) + r1[b, j, 2].astype(F32)
        part2[b, j] = total.astype(BF16)
        for d in (1, 2, 3):
            if first_axis(j) == "y":
                send(("r2", b, j), part2.at[b, j, :, (x + d) % 4], r2.at[b, j, d - 1], at_x(d))
            else:
                send(("r2", b, j), part2.at[b, j, :, (y + d) % 4], r2.at[b, j, d - 1], at_y(d))

    def reduce_h(b, j):
        arrived(("r2", b, j))
        own = part2[b, j, :, x] if first_axis(j) == "y" else part2[b, j, :, y]
        total = own.astype(F32) + r2[b, j, 0].astype(F32)
        total = total + r2[b, j, 1].astype(F32) + r2[b, j, 2].astype(F32)
        part3[b, j] = total.astype(BF16)
        send(("r3", b, j), part3.at[b, j], r3.at[b, j], at_h)

    def solved(b, j):
        arrived(("r3", b, j))
        value = (part3[b, j].astype(F32) + r3[b, j].astype(F32)).astype(BF16)
        xs[b, j, :, x, y] = value
        pot_ref[b, :, cols(j)] = xs[b, j, h, x, y]
        block = xs.at[b, j, :, x, y]
        for d in (1, 2, 3):
            send(("g2", b, j), block, block, at_x(d) if first_axis(j) == "y" else at_y(d))

    def gather_first(b, j):
        arrived(("g2", b, j))
        for d in (1, 2, 3):
            if first_axis(j) == "y":
                send(("g1", b, j), xs.at[b, j, :, :, y], xs.at[b, j, :, :, y], at_y(d))
            else:
                send(("g1", b, j), xs.at[b, j, :, x], xs.at[b, j, :, x], at_x(d))

    def couple(j):
        arrived(("g1", 1, j))
        value = jnp.dot(coup_ref[...], xs[1, j].reshape(512, w), preferred_element_type=F32)
        cpart[j] = value.astype(BF16).reshape(4, 2, 16, w)
        send(("c1", j), cpart.at[j, :, 1 - k], cr1.at[j], sibling)

    def couple_z(j):
        arrived(("c1", j))
        cp2[j] = (cpart[j, :, k].astype(F32) + cr1[j].astype(F32)).astype(BF16)
        for d in (1, 2, 3):
            send(("c2", j), cp2.at[j, (zl + d) % 4], cr2.at[j, d - 1], at_z(d))

    def reduced(j):
        arrived(("c2", j))
        carried = cp2[j, zl].astype(F32) + cr2[j, 0].astype(F32)
        carried = carried + cr2[j, 1].astype(F32) + cr2[j, 2].astype(F32)
        g[0, j, zl, k] = (rhsw_ref[0, :, cols(j)].astype(F32) - carried).astype(BF16)
        gather_z(0, j)

    def above(j):
        arrived(("g1", 0, j))

        def tile(t, carry):
            rows = pl.ds(pl.multiple_of(t * 192, 192), 192)
            value = jnp.dot(panel_ref[0, rows, :], xs[0, j].reshape(512, w), preferred_element_type=F32)
            value += jnp.dot(panel_ref[1, rows, :], xs[1, j].reshape(512, w), preferred_element_type=F32)
            fpart[j, t // 2, t % 2] = value.astype(BF16)
            return carry

        lax.fori_loop(0, 8, tile, 0)
        send(("f1", j), fpart.at[j, :, 1 - k], fr1.at[j], sibling)
        value = jnp.dot(modes_ref[0], xs[0, j].reshape(512, w), preferred_element_type=F32)
        value += jnp.dot(modes_ref[1], xs[1, j].reshape(512, w), preferred_element_type=F32)
        fo[:, cols(j)] = value

    def above_z(j):
        arrived(("f1", j))

        def tile(t, carry):
            fp2[j, t] = (fpart[j, t, k].astype(F32) + fr1[j, t].astype(F32)).astype(BF16)
            return carry

        lax.fori_loop(0, 4, tile, 0)
        for d in (2, 1, 3):
            send(("f2", j), fp2.at[j, (zl + d) % 4], fr2.at[j, d - 1], at_z(d))

    def above_end(j):
        arrived(("f2", j))
        total = fp2[j, zl].astype(F32) + fr2[j, 0].astype(F32)
        total = total + fr2[j, 1].astype(F32) + fr2[j, 2].astype(F32)
        above_ref[:, cols(j)] = rhsa_ref[:, cols(j)].astype(F32) - total

    def forces_core():
        for m in range(16):
            for n in range(8):
                fot[pl.ds(m * 8 + n, 1), :] = fo[pl.ds(m, 1), pl.ds(n * 128, 128)]
        fob[...] = fot[...].astype(BF16).reshape(4, 2, 16, 128)
        send("o1", fob.at[:, 1 - k], fob1, sibling)

    def forces_z():
        arrived("o1")
        fo2[...] = (fob[:, k].astype(F32) + fob1[...].astype(F32)).astype(BF16)
        for d in (1, 2, 3):
            send("o2", fo2.at[(zl + d) % 4], fo2r.at[d - 1], at_z(d))

    def forces_end():
        arrived("o2")
        total = fo2[zl].astype(F32) + fo2r[0].astype(F32)
        fin[...] = total + fo2r[1].astype(F32) + fo2r[2].astype(F32)
        for m in range(2):
            for n in range(8):
                forces_ref[pl.ds(m, 1), pl.ds(n * 128, 128)] = fin[pl.ds(m * 8 + n, 1), :]

    last = CHUNKS - 1
    plan = []
    for j in range(CHUNKS):
        steps = [functools.partial(load_rhs, j)]
        for b in (1, 0):
            for step in (gather_core, solve, reduce_second, reduce_h, solved, gather_first):
                steps.append(functools.partial(step, b, j))
            if b == 1:
                steps += [functools.partial(step, j) for step in (couple, couple_z, reduced)]
        steps.append(functools.partial(above, j))
        for s, step in enumerate(steps):
            plan.append((s + SKEW * j, j, step))
        base = len(steps)
        plan.append((base + SKEW * j, j, functools.partial(above_z, j)))
        plan.append((base + 1 + SKEW * j, j, functools.partial(above_end, j)))
        if j == last:
            plan.append((base - 0.5 + SKEW * j, j, forces_core))
            plan.append((base + 0.5 + SKEW * j, j, forces_z))
            plan.append((base + 1.5 + SKEW * j, j, forces_end))
    for _, _, step in sorted(plan, key=lambda item: (item[0], item[1])):
        step()
    for copy in sent:
        copy.wait_send()


def body(inverse, coupling, panel, modes, rhs_window, rhs_above):
    n, w = CHUNKS, 1024 // CHUNKS
    vmem = pl.BlockSpec(memory_space=pltpu.VMEM)

    def buf(*shape):
        return pltpu.VMEM(shape, BF16)

    return tuple(pl.pallas_call(
        kernel,
        out_shape=(
            jax.ShapeDtypeStruct((2, 16, 1024), BF16),
            jax.ShapeDtypeStruct((192, 1024), F32),
            jax.ShapeDtypeStruct((2, 1024), F32),
        ),
        in_specs=[vmem] * 6,
        out_specs=(vmem,) * 3,
        scratch_shapes=[
            buf(2, n, 4, 2, 16, w),
            buf(2, n, 2, 4, 4, 16, w),
            buf(2, n, 3, 2, 4, 16, w),
            buf(2, n, 2, 4, 16, w),
            buf(2, n, 3, 2, 16, w),
            buf(2, n, 2, 16, w),
            buf(2, n, 2, 16, w),
            buf(2, n, 2, 4, 4, 16, w),
            buf(n, 4, 2, 16, w),
            buf(n, 4, 16, w),
            buf(n, 4, 16, w),
            buf(n, 3, 16, w),
            buf(n, 4, 2, 192, w),
            buf(n, 4, 192, w),
            buf(n, 4, 192, w),
            buf(n, 3, 192, w),
            pltpu.VMEM((16, 1024), F32),
            pltpu.VMEM((128, 128), F32),
            buf(4, 2, 16, 128),
            buf(4, 16, 128),
            buf(4, 16, 128),
            buf(3, 16, 128),
            pltpu.VMEM((16, 128), F32),
            pltpu.SemaphoreType.DMA((N_SEMS,)),
            pltpu.SemaphoreType.DMA((N_SEMS,)),
        ],
        compiler_params=pltpu.CompilerParams(
            collective_id=0, has_side_effects=True, vmem_limit_bytes=48 * 2**20
        ),
        cost_estimate=pl.CostEstimate(
            flops=3_700_000_000, bytes_accessed=6_000_000, transcendentals=0
        ),
    )(inverse, coupling, panel, modes, rhs_window, rhs_above))


def solution(mesh):
    placed = (
        P(None, "pcol", "prow"),
        P("prow", "pcol"),
        P(None, "prow", "pcol"),
        P(None, "prow", "pcol"),
        P(None, ("prow", "pcol"), None),
        P(("prow", "pcol"), None),
    )
    return jax.shard_map(
        body,
        mesh=mesh,
        in_specs=placed,
        out_specs=(
            P(None, ("pcol", "prow"), None),
            P(("prow", "pcol"), None),
            P(("prow", "pcol"), None),
        ),
        check_vma=False,
    )
```

time: 794 us -> 130 us (0.16)
  waiting for transfers between devices: 677 us -> 0 us
  Pallas kernels: 0 us -> 120 us
  blocking collectives: 61.8 us -> 0 us
  matrix products: 17.5 us -> 0 us
  between operations: 14.9 us -> 0.65 us
    reduce_scatter x3 -> x0, waiting for transfers between devices: 437 us -> none  [the longest x2 408 us: solve_block(): lax.psum_scatter(jnp.dot(picked, across, preferred_element_type=jnp.float...]
    all_gather x2 -> x0, waiting for transfers between devices: 192 us -> none  [spread(): return lax.all_gather(solved, 'prow', axis=0, tiled=True)]
    pallas_call x0 -> x1, Pallas kernels: none -> 120 us  [body(): pl.pallas_call(kernel, out_shape=(jax.ShapeDtypeStruct((2, 16, 1024), BF1...]
    unnamed x9 -> x0, waiting for transfers between devices: 47.8 us -> none
    all_gather x2 -> x0, blocking collectives: 35.1 us -> none  [solve_block(): across = lax.all_gather(rhs_local, 'pcol', axis=0, tiled=True)]
    unnamed x1 -> x0, blocking collectives: 26.7 us -> none
    dot_general x7 -> x0, matrix products: 17.5 us -> none  [the longest x2 10.2 us: panel_term(): return jnp.dot(picked, columns, preferred_element_type=jnp.float32)]
  transfers between devices with their start and end apart: 7 -> 0, of which waited for: 7 -> 0; matrix products, arithmetic and copies ran while one was open for 3% -> 0% of each run, Pallas kernels for 0% -> 0%
where the time goes in v1:
time: 130 us; the launch traced here: 129 us
  Pallas kernels  120 us (92%)
  local copies, waits for them, and re-layouts  8.44 us (6%)
    pallas_call x1, Pallas kernels, body(): pl.pallas_call(kernel, out_shape=(jax.ShapeDtypeStruct((2, 16, 1024), BF1...  120 us
    unnamed x15, local copies, waits for them, and re-layouts  8.44 us

profile of v1, /device:TPU:1, one launch (start us, length us, event | category | flops | bytes accessed | tf_op | source)
XLA Modules:
  0.0 128.9 jit_solution(8082729372461108748)
XLA Ops:
  0.6 0.0 copy-start
  0.6 1.9 %copy-done = bf16[2,1536,512]{2,1,0:T(8,128)(2,1)S(1)} copy-done((bf16[2,1536,512]{2,1,0:T(8,128)(2,1)S(1)}, bf16[2,1536,512]{2,1,0:T(8,128)(2,1)}, u32[]{:S(2)}) %copy-start) | copy-done | bytes 3145752
  2.5 0.0 copy-start.1
  2.5 1.0 copy-done.1
  3.5 0.0 copy-start.2
  3.5 0.9 copy-done.2
  4.5 0.0 copy-start.3
  4.5 0.9 copy-done.3
  5.4 0.0 copy-start.4
  5.4 0.8 copy-done.4
  6.2 0.0 copy-start.5
  6.2 0.8 copy-done.5
  7.0 119.8 %shard_map.85 = (bf16[2,16,1024]{2,1,0:T(8,128)(2,1)S(1)}, f32[192,1024]{1,0:T(8,128)S(1)}, f32[2,1024]{1,0:T(2,128)S(1)}) custom-call(bf16[2,512,128]{2,1,0:T(8,128)(2,1)S(1)} %copy-done.2, bf16[128,512]{1,0:T(8,128)(2,1)S(1)} %copy-done.3, bf16[2,1536,512]{2,1,0:T(8,128)(2,1)S(1)} %copy-done, bf16[2,16,512]{2,1,0:T(8,128)(2,1)S(1)} %copy-done.5, ...), custom_call_target="tpu_custom_call" | custom-call | flops 3700000000 | bytes 6000000 | tf_op jit(solution)/shard_map/pallas_call | solution.py:244
  126.8 0.6 copy.12
  127.4 0.9 copy.13
  128.3 0.6 copy.14
Async XLA Ops:
  0.6 1.9 %copy-start = (bf16[2,1536,512]{2,1,0:T(8,128)(2,1)S(1)}, bf16[2,1536,512]{2,1,0:T(8,128)(2,1)}, u32[]{:S(2)}) copy-start(bf16[2,1536,512]{2,1,0:T(8,128)(2,1)} %panel_ref.1) | copy-start | bytes 9437188
  2.5 1.0 copy-start.1
  3.5 0.9 copy-start.2
  4.5 0.9 copy-start.3
  5.4 0.8 copy-start.4
  6.2 0.8 copy-start.5

commit v2 on v1

--- a/solution.py
+++ b/solution.py
@@ -10,19 +10,40 @@
 MESH = pl.DeviceIdType.MESH
 CHUNKS = 4
 SKEW = 0.0
+GROUP = 4
+TAIL = 0.1
+LATE = 0.0
 N_SEMS = 4 * 60 + 16
 BF16 = jnp.bfloat16
 F32 = jnp.float32
 
 
 def kernel(
-    inv_ref, coup_ref, panel_ref, modes_ref, rhsw_ref, rhsa_ref,
+    inv_hbm, coup_hbm, panel_hbm, modes_hbm, rhsw_hbm, rhsa_hbm,
     pot_ref, above_ref, forces_ref,
     g, part, r1, part2, r2, part3, r3, xs, cpart, cr1, cp2, cr2,
     fpart, fr1, fp2, fr2, fo, fot, fob, fob1, fo2, fo2r, fin,
-    send_sems, recv_sems,
+    inv_ref, coup_ref, panel_ref, modes_ref, rhsw_ref, rhsa_ref,
+    load_sems, send_sems, recv_sems, fm, f2_send, f2_recv,
 ):
     w = g.shape[-1]
+    loads = {}
+    for name, src, dst in (
+        ("rhsw", rhsw_hbm, rhsw_ref),
+        ("inv", inv_hbm, inv_ref),
+        ("coup", coup_hbm, coup_ref),
+        ("panel", panel_hbm, panel_ref),
+        ("modes", modes_hbm, modes_ref),
+        ("rhsa", rhsa_hbm, rhsa_ref),
+    ):
+        loads[name] = pltpu.make_async_copy(src, dst, load_sems.at[len(loads)])
+        loads[name].start()
+
+    def loaded(*names):
+        for name in names:
+            if name in loads:
+                loads.pop(name).wait()
+
     row = lax.axis_index("prow")
     col = lax.axis_index("pcol")
     h, x, y = row // 16, (row // 4) % 4, row % 4
@@ -36,6 +57,10 @@
 
     def at_z(d):
         return (row, ((zl + d) % 4) * 2 + k)
+
+    outer = jnp.logical_or(zl == 0, zl == 3)
+    near = jnp.where(zl < 2, 1 - zl, 5 - zl)
+    far = 3 - near
 
     at_h = ((1 - h) * 16 + x * 4 + y, col)
     sibling = (row, zl * 2 + 1 - k)
@@ -75,6 +100,7 @@
             send(("gz", b, j), g.at[b, j, zl, k], g.at[b, j, zl, k], at_z(d))
 
     def load_rhs(j):
+        loaded("rhsw")
         g[1, j, zl, k] = rhsw_ref[1, :, cols(j)]
         gather_z(1, j)
 
@@ -83,6 +109,7 @@
         send(("gc", b, j), g.at[b, j, :, k], g.at[b, j, :, k], sibling)
 
     def solve(b, j):
+        loaded("inv")
         arrived(("gc", b, j))
         right = g[b, j].reshape(128, w)
 
@@ -137,6 +164,7 @@
                 send(("g1", b, j), xs.at[b, j, :, x], xs.at[b, j, :, x], at_x(d))
 
     def couple(j):
+        loaded("coup")
         arrived(("g1", 1, j))
         value = jnp.dot(coup_ref[...], xs[1, j].reshape(512, w), preferred_element_type=F32)
         cpart[j] = value.astype(BF16).reshape(4, 2, 16, w)
@@ -156,6 +184,7 @@
         gather_z(0, j)
 
     def above(j):
+        loaded("panel", "modes")
         arrived(("g1", 0, j))
 
         def tile(t, carry):
@@ -179,14 +208,46 @@
             return carry
 
         lax.fori_loop(0, 4, tile, 0)
-        for d in (2, 1, 3):
-            send(("f2", j), fp2.at[j, (zl + d) % 4], fr2.at[j, d - 1], at_z(d))
+        @pl.when(outer)
+        def _():
+            f2_copy(j, 0, fp2.at[j, 3 - zl], fm.at[j], 3, near).start()
+            f2_copy(j, 1, fp2.at[j, far], fr2.at[j, 2], 2, far).start()
+            f2_copy(j, 2, fp2.at[j, near], fr2.at[j, 1], 1, near).start()
+            fr2[j, 2] = jnp.zeros_like(fr2[j, 2])
+
+        @pl.when(jnp.logical_not(outer))
+        def _():
+            f2_copy(j, 0, fp2.at[j, 3 - zl], fr2.at[j, 0], 0, 3 - zl).start()
+            f2_copy(j, 1, fp2.at[j, near], fr2.at[j, 0], 0, near).start()
+
+    def f2_copy(j, slot, src, dst, landing, line):
+        return pltpu.make_async_remote_copy(
+            src_ref=src, dst_ref=dst, send_sem=f2_send.at[j, slot], recv_sem=f2_recv.at[j, landing],
+            device_id=(row, line * 2 + k), device_id_type=MESH,
+        )
+
+    def above_merge(j):
+        @pl.when(jnp.logical_not(outer))
+        def _():
+            f2_copy(j, 0, fp2.at[j, far], fm.at[j], 3, far).wait_recv()
+            merged = fp2[j, far].astype(F32) + fm[j].astype(F32)
+            fp2[j, far] = merged.astype(BF16)
+            f2_copy(j, 2, fp2.at[j, far], fr2.at[j, 1], 1, far).start()
 
     def above_end(j):
-        arrived(("f2", j))
+        loaded("rhsa")
+        f2_copy(j, 0, fp2.at[j, zl], fr2.at[j, 0], 0, near).wait_recv()
+        f2_copy(j, 0, fp2.at[j, zl], fr2.at[j, 1], 1, near).wait_recv()
+
+        @pl.when(jnp.logical_not(outer))
+        def _():
+            f2_copy(j, 0, fp2.at[j, zl], fr2.at[j, 2], 2, near).wait_recv()
+
         total = fp2[j, zl].astype(F32) + fr2[j, 0].astype(F32)
         total = total + fr2[j, 1].astype(F32) + fr2[j, 2].astype(F32)
         above_ref[:, cols(j)] = rhsa_ref[:, cols(j)].astype(F32) - total
+        for slot in range(3):
+            f2_copy(j, slot, fp2.at[j, zl], fr2.at[j, 0], 0, near).wait_send()
 
     def forces_core():
         for m in range(16):
@@ -210,6 +271,10 @@
                 forces_ref[pl.ds(m, 1), pl.ds(n * 128, 128)] = fin[pl.ds(m * 8 + n, 1), :]
 
     last = CHUNKS - 1
+
+    def lag(j):
+        return SKEW * (j // GROUP)
+
     plan = []
     for j in range(CHUNKS):
         steps = [functools.partial(load_rhs, j)]
@@ -220,14 +285,18 @@
                 steps += [functools.partial(step, j) for step in (couple, couple_z, reduced)]
         steps.append(functools.partial(above, j))
         for s, step in enumerate(steps):
-            plan.append((s + SKEW * j, j, step))
+            s += TAIL * (j % GROUP) * (s == len(steps) - 1)
+            plan.append((s + lag(j), j, step))
         base = len(steps)
-        plan.append((base + SKEW * j, j, functools.partial(above_z, j)))
-        plan.append((base + 1 + SKEW * j, j, functools.partial(above_end, j)))
+        early = LATE * (j // GROUP < last // GROUP)
+        start = base - 1 + TAIL * (j % GROUP + 1.5) + lag(j) + early
+        plan.append((start, j, functools.partial(above_z, j)))
+        plan.append((start + TAIL * 1.2, j, functools.partial(above_merge, j)))
+        plan.append((base + 1 + lag(j), j, functools.partial(above_end, j)))
         if j == last:
-            plan.append((base - 0.5 + SKEW * j, j, forces_core))
-            plan.append((base + 0.5 + SKEW * j, j, forces_z))
-            plan.append((base + 1.5 + SKEW * j, j, forces_end))
+            plan.append((base - 1 + TAIL * GROUP + lag(j), j, forces_core))
+            plan.append((base + 0.5 + lag(j), j, forces_z))
+            plan.append((base + 1.5 + lag(j), j, forces_end))
     for _, _, step in sorted(plan, key=lambda item: (item[0], item[1])):
         step()
     for copy in sent:
@@ -248,7 +317,7 @@
             jax.ShapeDtypeStruct((192, 1024), F32),
             jax.ShapeDtypeStruct((2, 1024), F32),
         ),
-        in_specs=[vmem] * 6,
+        in_specs=[pl.BlockSpec(memory_space=pl.ANY)] * 6,
         out_specs=(vmem,) * 3,
         scratch_shapes=[
             buf(2, n, 4, 2, 16, w),
@@ -274,11 +343,21 @@
             buf(4, 16, 128),
             buf(3, 16, 128),
             pltpu.VMEM((16, 128), F32),
+            buf(2, 512, 128),
+            buf(128, 512),
+            buf(2, 1536, 512),
+            buf(2, 16, 512),
+            buf(2, 16, 1024),
+            buf(192, 1024),
+            pltpu.SemaphoreType.DMA((6,)),
             pltpu.SemaphoreType.DMA((N_SEMS,)),
             pltpu.SemaphoreType.DMA((N_SEMS,)),
+            buf(n, 192, w),
+            pltpu.SemaphoreType.DMA((n, 3)),
+            pltpu.SemaphoreType.DMA((n, 4)),
         ],
         compiler_params=pltpu.CompilerParams(
-            collective_id=0, has_side_effects=True, vmem_limit_bytes=48 * 2**20
+            collective_id=0, has_side_effects=True, vmem_limit_bytes=60 * 2**20
         ),
         cost_estimate=pl.CostEstimate(
             flops=3_700_000_000, bytes_accessed=6_000_000, transcendentals=0

time: 130 us -> 119 us (0.915)
  Pallas kernels: 120 us -> 113 us
  local copies, waits for them, and re-layouts: 8.44 us -> 4.86 us
    pallas_call x1, Pallas kernels: 120 us -> 113 us  [body(): pl.pallas_call(kernel, out_shape=(jax.ShapeDtypeStruct((2, 16, 1024), BF1...]
    unnamed x15 -> x3, local copies, waits for them, and re-layouts: 8.44 us -> 4.86 us
where the time goes in v2:
time: 119 us; the launch traced here: 118 us
  Pallas kernels  113 us (95%)
  local copies, waits for them, and re-layouts  4.86 us (4%)
    pallas_call x1, Pallas kernels, body(): pl.pallas_call(kernel, out_shape=(jax.ShapeDtypeStruct((2, 16, 1024), BF1...  113 us
    unnamed x3, local copies, waits for them, and re-layouts  4.86 us

profile of v2, /device:TPU:1, one launch (start us, length us, event | category | flops | bytes accessed | tf_op | source)
XLA Modules:
  0.0 118.3 jit_solution(17874957142720210856)
XLA Ops:
  0.6 112.8 %shard_map.85 = (bf16[2,16,1024]{2,1,0:T(8,128)(2,1)}, f32[192,1024]{1,0:T(8,128)}, f32[2,1024]{1,0:T(2,128)}) custom-call(bf16[2,512,128]{2,1,0:T(8,128)(2,1)} %inv_hbm.1, bf16[128,512]{1,0:T(8,128)(2,1)} %coup_hbm.1, bf16[2,1536,512]{2,1,0:T(8,128)(2,1)} %panel_hbm.1, bf16[2,16,512]{2,1,0:T(8,128)(2,1)} %modes_hbm.1, bf16[2,16,1024]{2,1,0:T(8,128)(2,1)} %rhsw_hbm.1, ...), custom_call_target="tpu_custom_call" | custom-call | flops 3700000000 | bytes 6000000 | tf_op jit(solution)/shard_map/pallas_call | solution.py:313
  113.4 1.5 %copy.12 = bf16[2,16,1024]{2,1,0:T(8,128)(2,1)} copy(bf16[2,16,1024]{2,1,0:T(8,128)(2,1)} %get-tuple-element.6) | data formatting | bytes 131072
  114.9 2.1 %copy.13 = f32[192,1024]{1,0:T(8,128)} copy(f32[192,1024]{1,0:T(8,128)} %get-tuple-element.7) | data formatting | bytes 1572864
  117.0 1.3 %copy.14 = f32[2,1024]{1,0:T(2,128)} copy(f32[2,1024]{1,0:T(2,128)} %get-tuple-element.8) | data formatting | bytes 16384

commit v3 on v2

v3 whole, which is shorter than its diff:
```python
import functools

import jax
import jax.numpy as jnp
from jax import lax
from jax.experimental import pallas as pl
from jax.experimental.pallas import tpu as pltpu
from jax.sharding import PartitionSpec as P

MESH = pl.DeviceIdType.MESH
CHUNKS = 2
HALF = 512
TAIL = 0.8
N_SEMS = 200
BF16 = jnp.bfloat16
F32 = jnp.float32


def kernel(
    inv_hbm, coup_hbm, panel_hbm, modes_hbm, rhsw_hbm, rhsa_hbm,
    pot_ref, above_ref, forces_ref,
    g, part, r1, part2, r2, xs, cpart, cr1, cp2, cr2,
    fpart, fr1, fp2, fr2, fo, fot, fob, fob1, fo2, fo2r, fin,
    inv2, coup2, panel_ref, modes_ref, rhsw_ref, rhsa_ref, rw0,
    load_sems, send_sems, recv_sems, fm, f2_send, f2_recv,
):
    w = g.shape[-1]
    row = lax.axis_index("prow")
    col = lax.axis_index("pcol")
    h, x, y = row // 16, (row // 4) % 4, row % 4
    zl, k = col // 2, col % 2

    loads = {}
    for name, src, dst in (
        ("rhsw", rhsw_hbm, rhsw_ref),
        ("inv1", inv_hbm.at[1], inv2.at[1, h]),
        ("coup", coup_hbm, coup2.at[h]),
        ("inv0", inv_hbm.at[0], inv2.at[0, h]),
        ("panel", panel_hbm, panel_ref),
        ("modes", modes_hbm, modes_ref),
        ("rhsa", rhsa_hbm, rhsa_ref),
    ):
        loads[name] = pltpu.make_async_copy(src, dst, load_sems.at[len(loads)])
        loads[name].start()

    def loaded(*names):
        for name in names:
            if name in loads:
                loads.pop(name).wait()

    def at_x(d):
        return (h * 16 + ((x + d) % 4) * 4 + y, col)

    def at_y(d):
        return (h * 16 + x * 4 + (y + d) % 4, col)

    def at_z(d):
        return (row, ((zl + d) % 4) * 2 + k)

    outer = jnp.logical_or(zl == 0, zl == 3)
    near = jnp.where(zl < 2, 1 - zl, 5 - zl)
    far = 3 - near

    def across_h(d):
        return ((1 - h) * 16 + x * 4 + y, ((zl + d) % 4) * 2 + k)

    at_h = ((1 - h) * 16 + x * 4 + y, col)
    sibling = (row, zl * 2 + 1 - k)

    barrier = pltpu.get_barrier_semaphore()
    partners = [at_x(d) for d in (1, 2, 3)] + [at_y(d) for d in (1, 2, 3)]
    partners += [at_z(d) for d in (1, 2, 3)] + [at_h, sibling]
    partners += [across_h(d) for d in (1, 2, 3)]
    for partner in partners:
        pl.semaphore_signal(barrier, inc=1, device_id=partner, device_id_type=MESH)
    pl.semaphore_wait(barrier, len(partners))

    sent = []
    pending = {}

    def send(key, src, dst, device):
        i = len(sent)
        copy = pltpu.make_async_remote_copy(
            src_ref=src, dst_ref=dst, send_sem=send_sems.at[i], recv_sem=recv_sems.at[i],
            device_id=device, device_id_type=MESH,
        )
        copy.start()
        sent.append(copy)
        pending.setdefault(key, []).append(copy)

    def arrived(key):
        for copy in pending.pop(key, ()):
            copy.wait_recv()

    def cols(half, j):
        return pl.ds(pl.multiple_of(half * HALF + j * w, 128), w)

    def first_axis(j):
        return "y" if j % 2 == 0 else "x"

    def load_rhs(j):
        loaded("rhsw")
        g[1, j, h, zl, k] = rhsw_ref[1, :, cols(h, j)]
        mine = g.at[1, j, h, zl, k]
        for d in (1, 2, 3):
            send(("gz", 1, j), mine, mine, at_z(d))
        for d in range(4):
            send(("gz", 1, j), rhsw_ref.at[1, :, cols(1 - h, j)], mine, across_h(d))

    def swap_inverse():
        send("inv1", inv_hbm.at[1], inv2.at[1, h], at_h)

    def swap_rhs():
        send("rw0", rhsw_ref.at[0, :, pl.ds(pl.multiple_of((1 - h) * HALF, 128), HALF)], rw0, at_h)

    def swap_coupling(part_no):
        rows = pl.ds(part_no * 32, 32)
        send("coup", coup_hbm.at[rows], coup2.at[h, rows], at_h)

    def swap_first(part_no):
        rows = pl.ds(part_no * 128, 128)
        send("inv0", inv_hbm.at[0, rows], inv2.at[0, h, rows], at_h)

    def gather_z(j):
        for d in (1, 2, 3):
            send(("gz", 0, j), g.at[0, j, :, zl, k], g.at[0, j, :, zl, k], at_z(d))

    def gather_core(b, j):
        arrived(("gz", b, j))
        send(("gc", b, j), g.at[b, j, :, :, k], g.at[b, j, :, :, k], sibling)

    def solve(b, j):
        loaded("inv%d" % b)
        arrived("inv%d" % b)
        arrived(("gc", b, j))
        right = g[b, j].reshape(2, 128, w)

        def tile(t, carry):
            rows = pl.ds(pl.multiple_of(t * 128, 128), 128)
            value = jnp.dot(inv2[b, 0, rows, :], right[0], preferred_element_type=F32)
            value += jnp.dot(inv2[b, 1, rows, :], right[1], preferred_element_type=F32)
            part[b, j, t // 2, pl.ds((t % 2) * 2, 2)] = value.astype(BF16).reshape(2, 4, 16, w)
            return carry

        lax.fori_loop(0, 4, tile, 0)
        for d in (1, 2, 3):
            if first_axis(j) == "y":
                send(("r1", b, j), part.at[b, j, :, :, (y + d) % 4], r1.at[b, j, d - 1], at_y(d))
            else:
                send(("r1", b, j), part.at[b, j, :, (x + d) % 4], r1.at[b, j, d - 1], at_x(d))

    def reduce_second(b, j):
        arrived(("r1", b, j))
        own = part[b, j, :, :, y] if first_axis(j) == "y" else part[b, j, :, x]
        total = own.astype(F32) + r1[b, j, 0].astype(F32)
        total = total + r1[b, j, 1].astype(F32) + r1[b, j, 2].astype(F32)
        part2[b, j] = total.astype(BF16)
        for d in (1, 2, 3):
            if first_axis(j) == "y":
                send(("r2", b, j), part2.at[b, j, :, (x + d) % 4], r2.at[b, j, d - 1], at_x(d))
            else:
                send(("r2", b, j), part2.at[b, j, :, (y + d) % 4], r2.at[b, j, d - 1], at_y(d))

    def spread_second(b, half, q, j):
        block = xs.at[b, half, j, :, x, y]
        for d in (1, 2, 3):
            send(("g2", b, q, j), block, block, at_x(d) if first_axis(j) == "y" else at_y(d))

    def solved(b, j):
        arrived(("r2", b, j))
        own = part2[b, j, :, x] if first_axis(j) == "y" else part2[b, j, :, y]
        total = own.astype(F32) + r2[b, j, 0].astype(F32)
        total = total + r2[b, j, 1].astype(F32) + r2[b, j, 2].astype(F32)
        xs[b, h, j, :, x, y] = total.astype(BF16)
        block = xs.at[b, h, j, :, x, y]
        if b == 0:
            send(("hh", b, j), block, block, at_h)
        spread_second(b, h, 0, j)
        if b == 1:
            send(("hh", b, j), block, block, at_h)
        pot_ref[b, :, cols(h, j)] = xs[b, h, j, h, x, y]

    def other_solved(b, j):
        arrived(("hh", b, j))
        spread_second(b, 1 - h, 1, j)
        pot_ref[b, :, cols(1 - h, j)] = xs[b, 1 - h, j, h, x, y]

    def gather_first(b, q, j):
        arrived(("g2", b, q, j))
        half = h if q == 0 else 1 - h
        for d in (1, 2, 3):
            if first_axis(j) == "y":
                block = xs.at[b, half, j, :, :, y]
                send(("g1", b, q, j), block, block, at_y(d))
            else:
                block = xs.at[b, half, j, :, x]
                send(("g1", b, q, j), block, block, at_x(d))

    def couple(j):
        loaded("coup")
        arrived("coup")
        arrived(("g1", 1, 0, j))
        right = xs[1, h, j].reshape(512, w)
        for side in range(2):
            value = jnp.dot(coup2[side], right, preferred_element_type=F32)
            cpart[j, side] = value.astype(BF16).reshape(4, 2, 16, w)
        send(("c1", j), cpart.at[j, :, :, 1 - k], cr1.at[j], sibling)

    def couple_z(j):
        arrived(("c1", j))
        cp2[j] = (cpart[j, :, :, k].astype(F32) + cr1[j].astype(F32)).astype(BF16)
        for d in (1, 2, 3):
            send(("c2", j), cp2.at[j, :, (zl + d) % 4], cr2.at[j, d - 1], at_z(d))

    def reduced(j):
        arrived(("c2", j))
        arrived("rw0")
        for side, rhs in ((h, rhsw_ref[0, :, cols(h, j)]), (1 - h, rw0[:, pl.ds(j * w, w)])):
            carried = cp2[j, side, zl].astype(F32) + cr2[j, 0, side].astype(F32)
            carried = carried + cr2[j, 1, side].astype(F32) + cr2[j, 2, side].astype(F32)
            g[0, j, side, zl, k] = (rhs.astype(F32) - carried).astype(BF16)
        gather_z(j)

    def above(q, i):
        j = q * CHUNKS + i
        half = h if q == 0 else 1 - h
        loaded("panel", "modes")
        arrived(("g1", 1, q, i))
        arrived(("g1", 0, q, i))

        def tile(t, carry):
            rows = pl.ds(pl.multiple_of(t * 192, 192), 192)
            value = jnp.dot(panel_ref[0, rows, :], xs[0, half, i].reshape(512, w), preferred_element_type=F32)
            value += jnp.dot(panel_ref[1, rows, :], xs[1, half, i].reshape(512, w), preferred_element_type=F32)
            fpart[j, t // 2, t % 2] = value.astype(BF16)
            return carry

        lax.fori_loop(0, 8, tile, 0)
        send(("f1", j), fpart.at[j, :, 1 - k], fr1.at[j], sibling)
        value = jnp.dot(modes_ref[0], xs[0, half, i].reshape(512, w), preferred_element_type=F32)
        value += jnp.dot(modes_ref[1], xs[1, half, i].reshape(512, w), preferred_element_type=F32)
        fo[:, cols(half, i)] = value

    def above_z(j):
        arrived(("f1", j))

        def tile(t, carry):
            fp2[j, t] = (fpart[j, t, k].astype(F32) + fr1[j, t].astype(F32)).astype(BF16)
            return carry

        lax.fori_loop(0, 4, tile, 0)
        @pl.when(outer)
        def _():
            f2_copy(j, 0, fp2.at[j, 3 - zl], fm.at[j], 3, near).start()
            f2_copy(j, 1, fp2.at[j, far], fr2.at[j, 2], 2, far).start()
            f2_copy(j, 2, fp2.at[j, near], fr2.at[j, 1], 1, near).start()
            fr2[j, 2] = jnp.zeros_like(fr2[j, 2])

        @pl.when(jnp.logical_not(outer))
        def _():
            f2_copy(j, 0, fp2.at[j, 3 - zl], fr2.at[j, 0], 0, 3 - zl).start()
            f2_copy(j, 1, fp2.at[j, near], fr2.at[j, 0], 0, near).start()

    def f2_copy(j, slot, src, dst, landing, line):
        return pltpu.make_async_remote_copy(
            src_ref=src, dst_ref=dst, send_sem=f2_send.at[j, slot], recv_sem=f2_recv.at[j, landing],
            device_id=(row, line * 2 + k), device_id_type=MESH,
        )

    def above_merge(j):
        @pl.when(jnp.logical_not(outer))
        def _():
            f2_copy(j, 0, fp2.at[j, far], fm.at[j], 3, far).wait_recv()
            merged = fp2[j, far].astype(F32) + fm[j].astype(F32)
            fp2[j, far] = merged.astype(BF16)
            f2_copy(j, 2, fp2.at[j, far], fr2.at[j, 1], 1, far).start()

    def above_end(j):
        loaded("rhsa")
        f2_copy(j, 0, fp2.at[j, zl], fr2.at[j, 0], 0, near).wait_recv()
        f2_copy(j, 0, fp2.at[j, zl], fr2.at[j, 1], 1, near).wait_recv()

        @pl.when(jnp.logical_not(outer))
        def _():
            f2_copy(j, 0, fp2.at[j, zl], fr2.at[j, 2], 2, near).wait_recv()

        total = fp2[j, zl].astype(F32) + fr2[j, 0].astype(F32)
        total = total + fr2[j, 1].astype(F32) + fr2[j, 2].astype(F32)
        here = cols(h if j < CHUNKS else 1 - h, j % CHUNKS)
        above_ref[:, here] = rhsa_ref[:, here].astype(F32) - total
        for slot in range(3):
            f2_copy(j, slot, fp2.at[j, zl], fr2.at[j, 0], 0, near).wait_send()

    def forces_core():
        for m in range(16):
            for n in range(8):
                fot[pl.ds(m * 8 + n, 1), :] = fo[pl.ds(m, 1), pl.ds(n * 128, 128)]
        fob[...] = fot[...].astype(BF16).reshape(4, 2, 16, 128)
        send("o1", fob.at[:, 1 - k], fob1, sibling)

    def forces_z():
        arrived("o1")
        fo2[...] = (fob[:, k].astype(F32) + fob1[...].astype(F32)).astype(BF16)
        for d in (1, 2, 3):
            send("o2", fo2.at[(zl + d) % 4], fo2r.at[d - 1], at_z(d))

    def forces_end():
        arrived("o2")
        total = fo2[zl].astype(F32) + fo2r[0].astype(F32)
        fin[...] = total + fo2r[1].astype(F32) + fo2r[2].astype(F32)
        for m in range(2):
            for n in range(8):
                forces_ref[pl.ds(m, 1), pl.ds(n * 128, 128)] = fin[pl.ds(m * 8 + n, 1), :]

    plan = []

    def at(place, step, *args):
        plan.append((place, len(plan), functools.partial(step, *args)))

    for j in range(CHUNKS):
        late = 0.1 * j
        at(0.0 + late, load_rhs, j)
        at(1.0 + late, gather_core, 1, j)
        at(2.0 + late, solve, 1, j)
        at(3.0 + late, reduce_second, 1, j)
        at(4.0 + late, solved, 1, j)
        at(5.0 + late, gather_first, 1, 0, j)
        at(6.0 + late, couple, j)
        at(6.5 + late, other_solved, 1, j)
        at(7.0 + late, couple_z, j)
        at(7.5 + late, gather_first, 1, 1, j)
        at(8.0 + late, reduced, j)
        at(9.0 + late, gather_core, 0, j)
        at(10.0 + late, solve, 0, j)
        at(11.0 + late, reduce_second, 0, j)
        at(12.0 + late, solved, 0, j)
        at(13.0 + late, gather_first, 0, 0, j)
        at(13.5 + late, other_solved, 0, j)
        at(14.05 + 0.01 * j, gather_first, 0, 1, j)
        for q in range(2):
            m = q * CHUNKS + j
            at(14.0 + q + late, above, q, j)
            place = 14.15 + q + late + (TAIL if m == CHUNKS - 1 else 0.0)
            at(place, above_z, m)
            at(place + 0.12, above_merge, m)
            at(16.5 + 0.1 * m, above_end, m)
    at(0.5, swap_inverse)
    at(0.6, swap_rhs)
    for i in range(4):
        at(2.5 + 0.5 * i, swap_coupling, i)
        at(4.5 + 0.5 * i, swap_first, i)
    at(15.0 + 0.1 * CHUNKS, forces_core)
    at(16.0, forces_z)
    at(17.0, forces_end)
    for _, _, step in sorted(plan, key=lambda item: (item[0], item[1])):
        step()
    assert not pending and len(sent) <= N_SEMS
    for copy in sent:
        copy.wait_send()


def body(inverse, coupling, panel, modes, rhs_window, rhs_above):
    n, w = CHUNKS, HALF // CHUNKS
    vmem = pl.BlockSpec(memory_space=pltpu.VMEM)

    def buf(*shape):
        return pltpu.VMEM(shape, BF16)

    return tuple(pl.pallas_call(
        kernel,
        out_shape=(
            jax.ShapeDtypeStruct((2, 16, 1024), BF16),
            jax.ShapeDtypeStruct((192, 1024), F32),
            jax.ShapeDtypeStruct((2, 1024), F32),
        ),
        in_specs=[pl.BlockSpec(memory_space=pl.ANY)] * 6,
        out_specs=(vmem,) * 3,
        scratch_shapes=[
            buf(2, n, 2, 4, 2, 16, w),
            buf(2, n, 2, 4, 4, 16, w),
            buf(2, n, 3, 2, 4, 16, w),
            buf(2, n, 2, 4, 16, w),
            buf(2, n, 3, 2, 16, w),
            buf(2, 2, n, 2, 4, 4, 16, w),
            buf(n, 2, 4, 2, 16, w),
            buf(n, 2, 4, 16, w),
            buf(n, 2, 4, 16, w),
            buf(n, 3, 2, 16, w),
            buf(2 * n, 4, 2, 192, w),
            buf(2 * n, 4, 192, w),
            buf(2 * n, 4, 192, w),
            buf(2 * n, 3, 192, w),
            pltpu.VMEM((16, 1024), F32),
            pltpu.VMEM((128, 128), F32),
            buf(4, 2, 16, 128),
            buf(4, 16, 128),
            buf(4, 16, 128),
            buf(3, 16, 128),
            pltpu.VMEM((16, 128), F32),
            buf(2, 2, 512, 128),
            buf(2, 128, 512),
            buf(2, 1536, 512),
            buf(2, 16, 512),
            buf(2, 16, 1024),
            buf(192, 1024),
            buf(16, HALF),
            pltpu.SemaphoreType.DMA((7,)),
            pltpu.SemaphoreType.DMA((N_SEMS,)),
            pltpu.SemaphoreType.DMA((N_SEMS,)),
            buf(2 * n, 192, w),
            pltpu.SemaphoreType.DMA((2 * n, 3)),
            pltpu.SemaphoreType.DMA((2 * n, 4)),
        ],
        compiler_params=pltpu.CompilerParams(
            collective_id=0, has_side_effects=True, vmem_limit_bytes=60 * 2**20
        ),
        cost_estimate=pl.CostEstimate(
            flops=3_700_000_000, bytes_accessed=6_000_000, transcendentals=0
        ),
    )(inverse, coupling, panel, modes, rhs_window, rhs_above))


def solution(mesh):
    placed = (
        P(None, "pcol", "prow"),
        P("prow", "pcol"),
        P(None, "prow", "pcol"),
        P(None, "prow", "pcol"),
        P(None, ("prow", "pcol"), None),
        P(("prow", "pcol"), None),
    )
    return jax.shard_map(
        body,
        mesh=mesh,
        in_specs=placed,
        out_specs=(
            P(None, ("pcol", "prow"), None),
            P(("prow", "pcol"), None),
            P(("prow", "pcol"), None),
        ),
        check_vma=False,
    )
```

time: 119 us -> 112 us (0.941)
  Pallas kernels: 113 us -> 106 us
    pallas_call x1, Pallas kernels: 113 us -> 106 us  [body(): pl.pallas_call(kernel, out_shape=(jax.ShapeDtypeStruct((2, 16, 1024), BF1...]
where the time goes in v3:
time: 112 us
  Pallas kernels  106 us (95%)
  local copies, waits for them, and re-layouts  4.86 us (4%)
    pallas_call x1, Pallas kernels, body(): pl.pallas_call(kernel, out_shape=(jax.ShapeDtypeStruct((2, 16, 1024), BF1...  106 us
    unnamed x3, local copies, waits for them, and re-layouts  4.86 us

profile of v3, /device:TPU:1, one launch (start us, length us, event | category | flops | bytes accessed | tf_op | source)
XLA Modules:
  0.0 111.7 jit_solution(6518668082016532927)
XLA Ops:
  0.6 106.2 %shard_map.85 = (bf16[2,16,1024]{2,1,0:T(8,128)(2,1)}, f32[192,1024]{1,0:T(8,128)}, f32[2,1024]{1,0:T(2,128)}) custom-call(bf16[2,512,128]{2,1,0:T(8,128)(2,1)} %inv_hbm.1, bf16[128,512]{1,0:T(8,128)(2,1)} %coup_hbm.1, bf16[2,1536,512]{2,1,0:T(8,128)(2,1)} %panel_hbm.1, bf16[2,16,512]{2,1,0:T(8,128)(2,1)} %modes_hbm.1, bf16[2,16,1024]{2,1,0:T(8,128)(2,1)} %rhsw_hbm.1, ...), custom_call_target="tpu_custom_call" | custom-call | flops 3700000000 | bytes 6000000 | tf_op jit(solution)/shard_map/pallas_call | solution.py:369
  106.8 1.5 %copy.12 = bf16[2,16,1024]{2,1,0:T(8,128)(2,1)} copy(bf16[2,16,1024]{2,1,0:T(8,128)(2,1)} %get-tuple-element.6) | data formatting | bytes 131072
  108.3 2.1 %copy.13 = f32[192,1024]{1,0:T(8,128)} copy(f32[192,1024]{1,0:T(8,128)} %get-tuple-element.7) | data formatting | bytes 1572864
  110.4 1.3 %copy.14 = f32[2,1024]{1,0:T(2,128)} copy(f32[2,1024]{1,0:T(2,128)} %get-tuple-element.8) | data formatting | bytes 16384

commit v4 on v3

--- a/solution.py
+++ b/solution.py
@@ -11,6 +11,8 @@
 CHUNKS = 2
 HALF = 512
 TAIL = 0.8
+PIECES = 16
+PLACES = (2.3, 2.3, 2.3, 3.3, 3.3, 3.3, 5.3, 5.3, 5.3, 10.3, 10.3, 10.3, 11.3, 11.3, 12.3, 12.3)
 N_SEMS = 200
 BF16 = jnp.bfloat16
 F32 = jnp.float32
@@ -22,7 +24,7 @@
     g, part, r1, part2, r2, xs, cpart, cr1, cp2, cr2,
     fpart, fr1, fp2, fr2, fo, fot, fob, fob1, fo2, fo2r, fin,
     inv2, coup2, panel_ref, modes_ref, rhsw_ref, rhsa_ref, rw0,
-    load_sems, send_sems, recv_sems, fm, f2_send, f2_recv,
+    load_sems, send_sems, recv_sems, fm, f2_send, f2_recv, ps_send, ps_recv,
 ):
     w = g.shape[-1]
     row = lax.axis_index("prow")
@@ -36,13 +38,19 @@
         ("inv1", inv_hbm.at[1], inv2.at[1, h]),
         ("coup", coup_hbm, coup2.at[h]),
         ("inv0", inv_hbm.at[0], inv2.at[0, h]),
-        ("panel", panel_hbm, panel_ref),
         ("modes", modes_hbm, modes_ref),
         ("rhsa", rhsa_hbm, rhsa_ref),
     ):
         loads[name] = pltpu.make_async_copy(src, dst, load_sems.at[len(loads)])
         loads[name].start()
 
+    ends = jnp.logical_or(zl == 0, zl == 3)
+    kept = pl.ds(pl.multiple_of((zl // 3) * 384, 128), 1152)
+    end_load = pltpu.make_async_copy(panel_hbm.at[:, kept], panel_ref.at[:, kept], load_sems.at[6])
+    full_load = pltpu.make_async_copy(panel_hbm, panel_ref, load_sems.at[6])
+    pl.when(ends)(end_load.start)
+    pl.when(jnp.logical_not(ends))(full_load.start)
+
     def loaded(*names):
         for name in names:
             if name in loads:
@@ -64,6 +72,7 @@
     def across_h(d):
         return ((1 - h) * 16 + x * 4 + y, ((zl + d) % 4) * 2 + k)
 
+    other_row = (1 - h) * 16 + x * 4 + y
     at_h = ((1 - h) * 16 + x * 4 + y, col)
     sibling = (row, zl * 2 + 1 - k)
 
@@ -116,6 +125,18 @@
     def swap_coupling(part_no):
         rows = pl.ds(part_no * 32, 32)
         send("coup", coup_hbm.at[rows], coup2.at[h, rows], at_h)
+
+    def panel_copy(piece):
+        count = 768 // PIECES
+        first = (piece * count) % 384
+        rows = pl.ds(pl.multiple_of((3 - zl) * 384 + first, 16), count)
+        return pltpu.make_async_remote_copy(
+            src_ref=panel_hbm.at[piece * count // 384, rows], dst_ref=panel_ref.at[piece * count // 384, rows],
+            send_sem=ps_send.at[piece], recv_sem=ps_recv.at[piece], device_id=at_h, device_id_type=MESH,
+        )
+
+    def swap_panel(piece):
+        pl.when(outer)(panel_copy(piece).start)
 
     def swap_first(part_no):
         rows = pl.ds(part_no * 128, 128)
@@ -224,7 +245,16 @@
     def above(q, i):
         j = q * CHUNKS + i
         half = h if q == 0 else 1 - h
-        loaded("panel", "modes")
+        loaded("modes")
+        if j == 0:
+            pl.when(outer)(end_load.wait)
+            pl.when(jnp.logical_not(outer))(full_load.wait)
+
+            @pl.when(outer)
+            def _():
+                for piece in range(PIECES):
+                    panel_copy(piece).wait_recv()
+
         arrived(("g1", 1, q, i))
         arrived(("g1", 0, q, i))
 
@@ -242,6 +272,7 @@
         fo[:, cols(half, i)] = value
 
     def above_z(j):
+        there = (j + CHUNKS) % (2 * CHUNKS)
         arrived(("f1", j))
 
         def tile(t, carry):
@@ -251,45 +282,46 @@
         lax.fori_loop(0, 4, tile, 0)
         @pl.when(outer)
         def _():
-            f2_copy(j, 0, fp2.at[j, 3 - zl], fm.at[j], 3, near).start()
-            f2_copy(j, 1, fp2.at[j, far], fr2.at[j, 2], 2, far).start()
-            f2_copy(j, 2, fp2.at[j, near], fr2.at[j, 1], 1, near).start()
-            fr2[j, 2] = jnp.zeros_like(fr2[j, 2])
+            f2_copy(j, 1, fp2.at[j, far], fm.at[j], 3, row, near).start()
+            f2_copy(j, 2, fp2.at[j, near], fr2.at[j, 1], 1, row, near).start()
+            f2_copy(j, 0, fp2.at[j, 3 - zl], fr2.at[there, 2], 2, other_row, 3 - zl, there).start()
 
         @pl.when(jnp.logical_not(outer))
         def _():
-            f2_copy(j, 0, fp2.at[j, 3 - zl], fr2.at[j, 0], 0, 3 - zl).start()
-            f2_copy(j, 1, fp2.at[j, near], fr2.at[j, 0], 0, near).start()
-
-    def f2_copy(j, slot, src, dst, landing, line):
+            f2_copy(j, 2, fp2.at[j, far], fr2.at[j, 1], 1, row, far).start()
+            f2_copy(j, 1, fp2.at[j, near], fr2.at[j, 0], 0, row, near).start()
+            fr2[j, 2] = jnp.zeros_like(fr2[j, 2])
+
+    def f2_copy(j, slot, src, dst, landing, to_row, line, there=None):
+        there = j if there is None else there
         return pltpu.make_async_remote_copy(
-            src_ref=src, dst_ref=dst, send_sem=f2_send.at[j, slot], recv_sem=f2_recv.at[j, landing],
-            device_id=(row, line * 2 + k), device_id_type=MESH,
+            src_ref=src, dst_ref=dst, send_sem=f2_send.at[j, slot], recv_sem=f2_recv.at[there, landing],
+            device_id=(to_row, line * 2 + k), device_id_type=MESH,
         )
 
     def above_merge(j):
         @pl.when(jnp.logical_not(outer))
         def _():
-            f2_copy(j, 0, fp2.at[j, far], fm.at[j], 3, far).wait_recv()
-            merged = fp2[j, far].astype(F32) + fm[j].astype(F32)
-            fp2[j, far] = merged.astype(BF16)
-            f2_copy(j, 2, fp2.at[j, far], fr2.at[j, 1], 1, far).start()
+            f2_copy(j, 0, fp2.at[j, far], fm.at[j], 3, row, near).wait_recv()
+            merged = fp2[j, 3 - zl].astype(F32) + fm[j].astype(F32)
+            fp2[j, 3 - zl] = merged.astype(BF16)
+            f2_copy(j, 0, fp2.at[j, 3 - zl], fr2.at[j, 0], 0, row, 3 - zl).start()
 
     def above_end(j):
         loaded("rhsa")
-        f2_copy(j, 0, fp2.at[j, zl], fr2.at[j, 0], 0, near).wait_recv()
-        f2_copy(j, 0, fp2.at[j, zl], fr2.at[j, 1], 1, near).wait_recv()
-
-        @pl.when(jnp.logical_not(outer))
+        f2_copy(j, 0, fp2.at[j, zl], fr2.at[j, 0], 0, row, near).wait_recv()
+        f2_copy(j, 0, fp2.at[j, zl], fr2.at[j, 1], 1, row, near).wait_recv()
+
+        @pl.when(outer)
         def _():
-            f2_copy(j, 0, fp2.at[j, zl], fr2.at[j, 2], 2, near).wait_recv()
+            f2_copy(j, 0, fp2.at[j, zl], fr2.at[j, 2], 2, row, near).wait_recv()
 
         total = fp2[j, zl].astype(F32) + fr2[j, 0].astype(F32)
         total = total + fr2[j, 1].astype(F32) + fr2[j, 2].astype(F32)
         here = cols(h if j < CHUNKS else 1 - h, j % CHUNKS)
         above_ref[:, here] = rhsa_ref[:, here].astype(F32) - total
         for slot in range(3):
-            f2_copy(j, slot, fp2.at[j, zl], fr2.at[j, 0], 0, near).wait_send()
+            f2_copy(j, slot, fp2.at[j, zl], fr2.at[j, 0], 0, row, near).wait_send()
 
     def forces_core():
         for m in range(16):
@@ -349,6 +381,8 @@
     for i in range(4):
         at(2.5 + 0.5 * i, swap_coupling, i)
         at(4.5 + 0.5 * i, swap_first, i)
+    for i in range(PIECES):
+        at(PLACES[i], swap_panel, i)
     at(15.0 + 0.1 * CHUNKS, forces_core)
     at(16.0, forces_z)
     at(17.0, forces_end)
@@ -357,6 +391,11 @@
     assert not pending and len(sent) <= N_SEMS
     for copy in sent:
         copy.wait_send()
+
+    @pl.when(outer)
+    def _():
+        for piece in range(PIECES):
+            panel_copy(piece).wait_send()
 
 
 def body(inverse, coupling, panel, modes, rhs_window, rhs_above):
@@ -410,6 +449,8 @@
             buf(2 * n, 192, w),
             pltpu.SemaphoreType.DMA((2 * n, 3)),
             pltpu.SemaphoreType.DMA((2 * n, 4)),
+            pltpu.SemaphoreType.DMA((PIECES,)),
+            pltpu.SemaphoreType.DMA((PIECES,)),
         ],
         compiler_params=pltpu.CompilerParams(
             collective_id=0, has_side_effects=True, vmem_limit_bytes=60 * 2**20

time: 112 us -> 110 us (0.982)
  Pallas kernels: 106 us -> 103 us
    pallas_call x1, Pallas kernels: 106 us -> 103 us  [body(): pl.pallas_call(kernel, out_shape=(jax.ShapeDtypeStruct((2, 16, 1024), BF1...]
where the time goes in v4:
time: 110 us; the launch traced here: 109 us
  Pallas kernels  103 us (94%)
  local copies, waits for them, and re-layouts  4.86 us (4%)
    pallas_call x1, Pallas kernels, body(): pl.pallas_call(kernel, out_shape=(jax.ShapeDtypeStruct((2, 16, 1024), BF1...  103 us
    unnamed x3, local copies, waits for them, and re-layouts  4.86 us

profile of v4, /device:TPU:1, one launch (start us, length us, event | category | flops | bytes accessed | tf_op | source)
XLA Modules:
  0.0 109.0 jit_solution(12636577338174708752)
XLA Ops:
  0.6 103.5 %shard_map.85 = (bf16[2,16,1024]{2,1,0:T(8,128)(2,1)}, f32[192,1024]{1,0:T(8,128)}, f32[2,1024]{1,0:T(2,128)}) custom-call(bf16[2,512,128]{2,1,0:T(8,128)(2,1)} %inv_hbm.1, bf16[128,512]{1,0:T(8,128)(2,1)} %coup_hbm.1, bf16[2,1536,512]{2,1,0:T(8,128)(2,1)} %panel_hbm.1, bf16[2,16,512]{2,1,0:T(8,128)(2,1)} %modes_hbm.1, bf16[2,16,1024]{2,1,0:T(8,128)(2,1)} %rhsw_hbm.1, ...), custom_call_target="tpu_custom_call" | custom-call | flops 3700000000 | bytes 6000000 | tf_op jit(solution)/shard_map/pallas_call | solution.py:408
  104.1 1.5 %copy.12 = bf16[2,16,1024]{2,1,0:T(8,128)(2,1)} copy(bf16[2,16,1024]{2,1,0:T(8,128)(2,1)} %get-tuple-element.6) | data formatting | bytes 131072
  105.6 2.1 %copy.13 = f32[192,1024]{1,0:T(8,128)} copy(f32[192,1024]{1,0:T(8,128)} %get-tuple-element.7) | data formatting | bytes 1572864
  107.7 1.3 %copy.14 = f32[2,1024]{1,0:T(2,128)} copy(f32[2,1024]{1,0:T(2,128)} %get-tuple-element.8) | data formatting | bytes 16384

commit v5 on v4

--- a/solution.py
+++ b/solution.py
@@ -275,22 +275,27 @@
         there = (j + CHUNKS) % (2 * CHUNKS)
         arrived(("f1", j))
 
-        def tile(t, carry):
+        def add(t):
             fp2[j, t] = (fpart[j, t, k].astype(F32) + fr1[j, t].astype(F32)).astype(BF16)
-            return carry
-
-        lax.fori_loop(0, 4, tile, 0)
+
         @pl.when(outer)
         def _():
+            add(far)
             f2_copy(j, 1, fp2.at[j, far], fm.at[j], 3, row, near).start()
+            add(near)
             f2_copy(j, 2, fp2.at[j, near], fr2.at[j, 1], 1, row, near).start()
+            add(3 - zl)
             f2_copy(j, 0, fp2.at[j, 3 - zl], fr2.at[there, 2], 2, other_row, 3 - zl, there).start()
 
         @pl.when(jnp.logical_not(outer))
         def _():
+            add(far)
             f2_copy(j, 2, fp2.at[j, far], fr2.at[j, 1], 1, row, far).start()
+            add(near)
             f2_copy(j, 1, fp2.at[j, near], fr2.at[j, 0], 0, row, near).start()
+            add(3 - zl)
             fr2[j, 2] = jnp.zeros_like(fr2[j, 2])
+        add(zl)
 
     def f2_copy(j, slot, src, dst, landing, to_row, line, there=None):
         there = j if there is None else there
@@ -383,8 +388,8 @@
         at(4.5 + 0.5 * i, swap_first, i)
     for i in range(PIECES):
         at(PLACES[i], swap_panel, i)
-    at(15.0 + 0.1 * CHUNKS, forces_core)
-    at(16.0, forces_z)
+    at(15.12, forces_core)
+    at(15.24, forces_z)
     at(17.0, forces_end)
     for _, _, step in sorted(plan, key=lambda item: (item[0], item[1])):
         step()

time: 110 us -> 109 us (level)
  no operation moved by 1% of the time
where the time goes in v5:
time: 109 us
  Pallas kernels  103 us (94%)
  local copies, waits for them, and re-layouts  4.86 us (4%)
    pallas_call x1, Pallas kernels, body(): pl.pallas_call(kernel, out_shape=(jax.ShapeDtypeStruct((2, 16, 1024), BF1...  103 us
    unnamed x3, local copies, waits for them, and re-layouts  4.86 us

profile of v5, /device:TPU:1, one launch (start us, length us, event | category | flops | bytes accessed | tf_op | source)
XLA Modules:
  0.0 108.5 jit_solution(8880610638140928534)
XLA Ops:
  0.6 103.1 %shard_map.85 = (bf16[2,16,1024]{2,1,0:T(8,128)(2,1)}, f32[192,1024]{1,0:T(8,128)}, f32[2,1024]{1,0:T(2,128)}) custom-call(bf16[2,512,128]{2,1,0:T(8,128)(2,1)} %inv_hbm.1, bf16[128,512]{1,0:T(8,128)(2,1)} %coup_hbm.1, bf16[2,1536,512]{2,1,0:T(8,128)(2,1)} %panel_hbm.1, bf16[2,16,512]{2,1,0:T(8,128)(2,1)} %modes_hbm.1, bf16[2,16,1024]{2,1,0:T(8,128)(2,1)} %rhsw_hbm.1, ...), custom_call_target="tpu_custom_call" | custom-call | flops 3700000000 | bytes 6000000 | tf_op jit(solution)/shard_map/pallas_call | solution.py:413
  103.7 1.5 %copy.12 = bf16[2,16,1024]{2,1,0:T(8,128)(2,1)} copy(bf16[2,16,1024]{2,1,0:T(8,128)(2,1)} %get-tuple-element.6) | data formatting | bytes 131072
  105.2 2.1 %copy.13 = f32[192,1024]{1,0:T(8,128)} copy(f32[192,1024]{1,0:T(8,128)} %get-tuple-element.7) | data formatting | bytes 1572864
  107.3 1.3 %copy.14 = f32[2,1024]{1,0:T(2,128)} copy(f32[2,1024]{1,0:T(2,128)} %get-tuple-element.8) | data formatting | bytes 16384
